TPU v7x, 32 devices: a whole 2x2x4 slice. The times are simulated.
32 devices in a mesh: groups: 2 (over y), band: 4 (over z), comp: 2 (over x), sub: 2 (over core).
Axes of the slice: x: 2, y: 2, z: 4, core: 2. Of those that a mesh axis runs over, the one named last changes fastest.
Arguments:
- orbitals: float32 [1024, 16384], P(('groups', 'band'), ('comp', 'sub')), parts along dimension 0, may hold values from -6 to 6
- potential: float32 [32768], P(('groups', 'comp', 'sub')), parts along dimension 0, may hold values from 0.5 to 8
- proj_values: float32 [64, 4, 1024], P('groups'), parts along dimension 0, may hold values from -6 to 6
- block_list: int32 [64, 8], P('groups'), parts along dimension 0, may hold values from 0 to 127
- proj_energy: float32 [64, 4], P('groups'), parts along dimension 0, may hold values from 4 to 32
Outputs:
- updated: float32 [1024, 16384], P(('groups', 'band'), ('comp', 'sub')), parts along dimension 0
There are 2 independent parts, one for each index of `groups`. A program takes and returns all parts, laid end to end along the dimension named above; each array names one. Nothing has to cross between parts.
Inputs may be any that keep to these rules, and one draw needn't show every extreme that they name: `block_list`: an atom's list may name a block more than once.
All inputs are finite; a program needn't handle non-finite values.
Results may differ from a plain program's by a relative error of at most 0.00014.
Values sent between devices are 32-bit elements; how exact they have to be, the bound alone decides.
A program may use at most 64 MiB of HBM per device.

v0:
```python
import math

import jax
import jax.numpy as jnp
from jax import lax
from jax.sharding import PartitionSpec as P

step_size = 0.5


def early_correlation(comp_psi, total_coef):
    highest = lax.Precision.HIGHEST
    s_part = jnp.dot(
        comp_psi, comp_psi.T, precision=highest, preferred_element_type=jnp.float32
    ) * (1.0 / total_coef)
    return s_part


def on_device(orbitals, potential, proj_values, block_list, proj_energy):
    highest = lax.Precision.HIGHEST
    part_count = lax.axis_size(("comp", "sub"))
    row_width = orbitals.shape[1]
    total_coef = row_width * part_count
    atom_count, proj_count, proj_len = proj_values.shape
    blk_count = block_list.shape[1]
    proj_norm = 1.0 / math.sqrt(proj_len)
    proj_four = proj_values.reshape(atom_count, proj_count, blk_count, 128)
    weighted = proj_four * proj_energy[:, :, None, None]
    tile_count = row_width // 128
    tiles = orbitals.reshape(orbitals.shape[0], tile_count, 128)
    local_idx = block_list - lax.axis_index(("comp", "sub")) * tile_count
    inside = ((local_idx >= 0) & (local_idx < tile_count)).astype(jnp.float32)
    safe_idx = jnp.clip(local_idx, 0, tile_count - 1)
    picked = tiles[:, safe_idx] * inside[None, :, :, None]
    partial_value = jnp.einsum("akbc,iabc->aki", proj_four, picked, precision=highest)
    coupling = lax.psum(partial_value, ("comp", "sub")) * proj_norm
    contrib = jnp.einsum("akbc,aki->iabc", weighted, coupling, precision=highest) * proj_norm
    contrib = contrib * inside[None, :, :, None]
    extra = jnp.zeros_like(tiles).at[:, safe_idx].add(contrib)
    hpsi = potential[None, :] * orbitals + extra.reshape(orbitals.shape)
    comp_psi, comp_hpsi = (
        lax.all_to_all(orbitals, "band", split_axis=1, concat_axis=0, tiled=True),
        lax.all_to_all(hpsi, "band", split_axis=1, concat_axis=0, tiled=True),
    )
    correlation = early_correlation(comp_psi, total_coef)
    h_part = jnp.dot(
        comp_psi, comp_hpsi.T, precision=highest, preferred_element_type=jnp.float32
    ) * (1.0 / total_coef)
    orb_count = comp_psi.shape[0]
    correlation, hmat = lax.psum((correlation, h_part), ("band", "comp", "sub"))
    identity = jnp.eye(orb_count, dtype=jnp.float32)
    lagrange = 0.5 * (hmat + hmat.T)
    orthogonal = 1.5 * identity - 0.5 * correlation
    mix_psi = jnp.dot(
        orthogonal,
        identity + step_size * lagrange,
        precision=highest,
        preferred_element_type=jnp.float32,
    )
    mix_h = -step_size * orthogonal
    result = jnp.dot(mix_psi, comp_psi, precision=highest, preferred_element_type=jnp.float32)
    result = result + jnp.dot(
        mix_h, comp_hpsi, precision=highest, preferred_element_type=jnp.float32
    )
    return lax.all_to_all(result, "band", split_axis=0, concat_axis=1, tiled=True)


def solution(mesh):
    in_specs = (
        P(("groups", "band"), ("comp", "sub")),
        P(("groups", "comp", "sub")),
        P("groups", None, None),
        P("groups", None),
        P("groups", None),
    )
    out_specs = P(("groups", "band"), ("comp", "sub"))
    return jax.shard_map(
        on_device, mesh=mesh, in_specs=in_specs, out_specs=out_specs, check_vma=False
    )
```

profile of v0, /device:TPU:14, one launch (start us, length us, event | category | flops | bytes accessed | tf_op | source)
XLA Modules:
  0.0 359.6 jit_solution(5834884739097825792)
XLA Ops:
  6.5 2.9 copy.22
  9.4 0.0 copy-start.3
  9.4 5.4 %all-to-all-start = ((f32[128,4,1024]{0,2,1:T(8,128)}), f32[128,4,1024]{0,2,1:T(8,128)}, u32[]{:S(2)}, u32[]{:S(2)}) async-start(f32[128,4,1024]{0,2,1:T(8,128)} %bitcast), calls=%async_computation | async-start | bytes 4194304 | tf_op jit(solution)/shard_map/all_to_all | solution.py:42
  14.9 0.0 all-reduce.4.cloned.1.call-start
  14.9 0.0 copy-done.3
  14.9 0.1 copy.25
  15.0 0.1 reshape.34
  15.0 1.9 copy.27
  17.0 0.1 copy.28
  17.1 0.0 copy-start
  17.1 7.4 %gather_fusion = f32[256,128,128]{2,1,0:T(8,128)} fusion(f32[128,32,128]{2,0,1:T(8,128)S(1)} %copy.27, s32[1024]{0:T(1024)S(1)} %pad_clamp_fusion), kind=kCustom, calls=%fused_computation | custom fusion | bytes 33555456 | tf_op jit(solution)/shard_map/gather | solution.py:34
  24.5 0.0 copy-done
  24.5 0.0 copy-start.4
  24.5 18.0 %fusion.5 = f32[32,4,128]{2,1,0:T(4,128)} fusion(f32[32,8,128,128]{3,2,1,0:T(8,128)} %bitcast.55, f32[32,8]{1,0:T(8,128)S(1)} %copy.28, f32[32,4,1024]{2,1,0:T(4,128)S(1)} %copy-done), kind=kOutput, calls=%fused_computation.12 | convolution fusion | flops 205520896 | bytes 17368064 | tf_op jit(solution)/shard_map/akbc,iabc->aki/dot_general | solution.py:35
  42.5 0.0 all-reduce.4.cloned.1.call-update
  42.5 0.1 copy.32
  42.6 0.0 copy-done.4
  42.6 0.1 copy.30
  42.7 30.9 %all-reduce.4.cloned.1.call-done = f32[32,4,128]{2,1,0:T(4,128)} async-done(((f32[32,4,128]{2,1,0:T(4,128)}), f32[32,4,128]{2,1,0:T(4,128)}) %all-reduce.4.cloned.1.call-update) | async-done | bytes 65552 | tf_op jit(solution)/shard_map/psum | solution.py:36
  73.6 18.6 %convolution_multiply_fusion = f32[32,128,8,128]{3,1,2,0:T(8,128)} fusion(f32[32,8]{1,0:T(8,128)S(1)} %copy.32, f32[32,4,1024]{2,1,0:T(4,128)S(1)} %copy-done, f32[32,4]{1,0:T(8,128)S(1)} %copy.30, f32[32,4,128]{2,1,0:T(4,128)} %all-reduce.4.cloned.1.call-done), kind=kOutput, calls=%fused_computation.5 | convolution fusion | flops 205668352 | bytes 17368576 | tf_op jit(solution)/shard_map/akbc,aki->iabc/dot_general | solution.py:37
  92.2 0.2 broadcast_in_dim.4
  92.4 33.1 %scatter_fusion = f32[128,32,128]{2,0,1:T(8,128)S(1)} fusion(f32[128,32,128]{2,0,1:T(8,128)S(1)} %broadcast_in_dim.4, s32[256]{0:T(256)S(1)} %reshape.34, f32[256,128,128]{2,1,0:T(8,128)} %bitcast.56), kind=kCustom, calls=%fused_computation.1 | custom fusion | flops 4194304 | bytes 50332672 | tf_op jit(solution)/shard_map/scatter-add | solution.py:39
  125.6 0.0 copy-start.2
  125.6 1.9 copy.33
  127.5 0.0 copy-done.2
  127.5 2.5 bitcast_add_fusion
  130.0 1.8 copy.34
  131.8 0.0 all-to-all-done
  131.8 5.1 %all-to-all-start.1 = ((f32[128,4,1024]{2,0,1:T(8,128)}), f32[128,4,1024]{2,0,1:T(8,128)}, u32[]{:S(2)}, u32[]{:S(2)}) async-start(f32[128,4,1024]{2,0,1:T(8,128)} %copy.34), calls=%async_computation.1 | async-start | bytes 4194304 | tf_op jit(solution)/shard_map/all_to_all | solution.py:43
  137.0 0.0 all-reduce.6.cloned.1.call-start
  137.0 2.1 copy.23
  139.1 4.5 %convolution_multiply_fusion.2 = f32[512,512]{1,0:T(8,128)} fusion(f32[512,1024]{1,0:T(8,128)S(1)} %bitcast.57), kind=kOutput, calls=%fused_computation.11 | convolution fusion | flops 3221487616 | bytes 3145728 | tf_op jit(solution)/shard_map/dot_general | solution.py:13
  143.6 37.8 %all-to-all-done.1 = f32[128,4,1024]{2,0,1:T(8,128)} async-done(((f32[128,4,1024]{2,0,1:T(8,128)}), f32[128,4,1024]{2,0,1:T(8,128)}, u32[]{:S(2)}, u32[]{:S(2)}) %all-to-all-start.1) | async-done | bytes 2097184 | tf_op jit(solution)/shard_map/all_to_all | solution.py:43
  181.3 6.1 %fusion.4 = f32[512,512]{0,1:T(8,128)} fusion(f32[512,1024]{1,0:T(8,128)} %bitcast.18, f32[512,1024]{1,0:T(8,128)S(1)} %bitcast.58), kind=kOutput, calls=%fused_computation.10 | convolution fusion | flops 3221487616 | bytes 5242880 | tf_op jit(solution)/shard_map/dot_general | solution.py:46
  187.4 0.0 all-reduce.6.cloned.1.call-update
  187.4 99.6 %all-reduce.6.cloned.1.call-done = (f32[512,512]{0,1:T(8,128)}, f32[512,512]{1,0:T(8,128)}) async-done(((f32[512,512]{0,1:T(8,128)}, f32[512,512]{1,0:T(8,128)}), (f32[512,512]{0,1:T(8,128)}, f32[512,512]{1,0:T(8,128)})) %all-reduce.6.cloned.1.call-update) | async-done | bytes 2097168 | tf_op jit(solution)/shard_map/psum | solution.py:50
  287.0 0.0 copy-start.1
  287.0 2.6 copy.35
  289.6 0.0 copy-done.1
  289.6 3.5 fusion.10
  293.2 3.8 %fusion.37 = f32[512,1024]{1,0:T(8,128)S(1)} fusion(f32[512,512]{1,0:T(8,128)S(1)} %fusion.10, f32[512,1024]{1,0:T(8,128)S(1)} %bitcast.59), kind=kOutput, calls=%fused_computation.49 | convolution fusion | flops 3221225472 | bytes 5242880 | tf_op jit(solution)/shard_map/dot_general | solution.py:61
  297.0 5.2 %convolution_add_fusion = f32[512,1024]{1,0:T(8,128)S(1)} fusion(f32[512,1024]{1,0:T(8,128)S(1)} %fusion.37, f32[512,1024]{1,0:T(8,128)} %bitcast.18, f32[512,512]{1,0:T(8,128)S(1)} %copy-done.1), kind=kOutput, calls=%fused_computation.8 | convolution fusion | flops 3223060480 | bytes 7340032 | tf_op jit(solution)/shard_map/dot_general | solution.py:62
  302.2 49.1 %all_to_all.57 = f32[4,128,1024]{2,1,0:T(8,128)S(1)} all-to-all(f32[4,128,1024]{2,1,0:T(8,128)S(1)} %bitcast.60), channel_id=1, replica_groups=mesh['groups'=2,'band'=4,'comp'=2,'sub'=2] {'band'}, dimensions={0} | all-to-all | bytes 4194304 | tf_op jit(solution)/shard_map/all_to_all | solution.py:65
  351.3 1.5 copy.39
  (4 shorter events, 0.0 us)
Async XLA Ops:
  9.4 5.5 %copy-start.3 = (s32[32,8]{0,1:T(8,128)S(1)}, s32[32,8]{0,1:T(8,128)}, u32[]{:S(2)}) copy-start(s32[32,8]{0,1:T(8,128)} %param.8) | copy-start | bytes 3076
  9.4 122.4 %all-to-all-start = ((f32[128,4,1024]{0,2,1:T(8,128)}), f32[128,4,1024]{0,2,1:T(8,128)}, u32[]{:S(2)}, u32[]{:S(2)}) async-start(f32[128,4,1024]{0,2,1:T(8,128)} %bitcast), calls=%async_computation | async-start | bytes 4194304 | tf_op jit(solution)/shard_map/all_to_all | solution.py:42
  14.9 58.7 %all-reduce.4.cloned.1.call-start = ((), (), s32[]{:S(2)}) async-start(), calls=%async_computation.3 | async-start | bytes 131072 | tf_op jit(solution)/shard_map/psum | solution.py:36
  17.1 7.4 %copy-start = (f32[32,4,1024]{2,1,0:T(4,128)S(1)}, f32[32,4,1024]{2,1,0:T(4,128)}, u32[]{:S(2)}) copy-start(f32[32,4,1024]{2,1,0:T(4,128)} %param.7) | copy-start | bytes 1572868
  24.5 18.1 %copy-start.4 = (f32[32,4]{0,1:T(4,128)S(1)}, f32[32,4]{0,1:T(4,128)}, u32[]{:S(2)}) copy-start(f32[32,4]{0,1:T(4,128)} %param.9) | copy-start | bytes 1540
  125.6 1.9 copy-start.2
  131.8 49.5 %all-to-all-start.1 = ((f32[128,4,1024]{2,0,1:T(8,128)}), f32[128,4,1024]{2,0,1:T(8,128)}, u32[]{:S(2)}, u32[]{:S(2)}) async-start(f32[128,4,1024]{2,0,1:T(8,128)} %copy.34), calls=%async_computation.1 | async-start | bytes 4194304 | tf_op jit(solution)/shard_map/all_to_all | solution.py:43
  137.0 150.0 %all-reduce.6.cloned.1.call-start = ((), (), s32[]{:S(2)}) async-start(), calls=%async_computation.4 | async-start | bytes 4194304 | tf_op jit(solution)/shard_map/psum | solution.py:50
  287.0 2.6 copy-start.1
Sparse Core Ops, SparseCore 0:
  42.6 30.9 all-reduce.3
  187.6 99.3 all-reduce.5
where the time goes:
time: 364 us; the launch traced here: 360 us
  waiting for transfers between devices  168 us (46%)
  matrix products  59.8 us (16%)
  blocking collectives  49.1 us (13%)
  other arithmetic  35.7 us (10%)
  local copies, waits for them, and re-layouts  22.7 us (6%)
  between operations  13.5 us (4%)
  starting transfers between devices  10.6 us (3%)
    psum x1, waiting for transfers between devices, on_device(): correlation, hmat = lax.psum((correlation, h_part), ('band', 'comp', 'sub'))  99.6 us
    all_to_all x1, blocking collectives, on_device(): lax.all_to_all(result, 'band', split_axis=0, concat_axis=1, tiled=True)  49.1 us
    all_to_all x1, waiting for transfers between devices, on_device(): lax.all_to_all(hpsi, 'band', split_axis=1, concat_axis=0, tiled=True)  37.8 us
    scatter-add x1, other arithmetic, on_device(): extra = jnp.zeros_like(tiles).at[:, safe_idx].add(contrib)  33.1 us
    psum x1, waiting for transfers between devices, on_device(): coupling = lax.psum(partial_value, ('comp', 'sub')) * proj_norm  30.9 us
    dot_general x1, matrix products, on_device(): jnp.einsum('akbc,aki->iabc', weighted, coupling, precision=highest)  18.6 us
    dot_general x1, matrix products, on_device(): jnp.einsum('akbc,iabc->aki', proj_four, picked, precision=highest)  18 us
    gather x1, local copies, waits for them, and re-layouts, on_device(): picked = tiles[:, safe_idx] * inside[None, :, :, None]  7.37 us
  transfers between devices with their start and end apart: 4, of which 3 were waited for; matrix products, arithmetic and copies ran while one was open for 26% of the time, Pallas kernels for 0%

commit v1 on v0

v1 whole, which is shorter than its diff:
```python
import functools
import math

import jax
import jax.numpy as jnp
from jax import lax
from jax.experimental import pallas as pl
from jax.experimental.pallas import tpu as pltpu
from jax.sharding import PartitionSpec as P

step_size = 0.5
TILE = 128
CHUNK = 256
MESH = pl.DeviceIdType.MESH


def split(value):
    high = value.astype(jnp.bfloat16)
    low = (value - high.astype(jnp.float32)).astype(jnp.bfloat16)
    return high, low


def dot3(a, b, contract):
    dims = (((1,), (contract,)), ((), ()))
    one = functools.partial(
        lax.dot_general, dimension_numbers=dims, preferred_element_type=jnp.float32
    )
    return one(a[0], b[0]) + (one(a[0], b[1]) + one(a[1], b[0]))


def pair_index(i, j):
    return j * (j + 1) // 2 + i


def step_kernel(sizes, x_ref, v_ref, proj_ref, blk_ref, en_ref, out_ref,
                xs, y_hi, y_lo, red, fin, lm_hi, lm_lo, om_hi, om_lo, res,
                sub_box, comp_box, band_box, own_sem,
                in_send, in_recv, out_send, out_recv, keep_sem,
                rs_send, rs_recv, ag_send, ag_recv):
    nband, ncomp, nsub = sizes
    rows = x_ref.shape[0]
    norb, own = xs.shape
    nproj = proj_ref.shape[0]
    nblk = blk_ref.shape[1]
    chunks = own // CHUNK
    tri = norb // TILE
    pairs = tri * (tri + 1) // 2
    total_coef = own * nband * ncomp * nsub
    norm = 1.0 / math.sqrt(nblk * TILE)
    band = lax.axis_index("band")
    comp = lax.axis_index("comp")
    sub = lax.axis_index("sub")
    axes = {"band": (nband, band), "comp": (ncomp, comp), "sub": (nsub, sub)}

    barrier = pltpu.get_barrier_semaphore()
    for name, (count, me) in axes.items():
        for d in range(1, count):
            pl.semaphore_signal(barrier, inc=1, device_id={name: lax.rem(me + d, count)},
                                device_id_type=MESH)
    pl.semaphore_wait(barrier, nband + ncomp + nsub - 3)

    def cols_at(k):
        return pl.ds(pl.multiple_of(k * CHUNK, CHUNK), CHUNK)

    def wide_at(owner, k):
        return pl.ds(pl.multiple_of(owner * own + k * CHUNK, CHUNK), CHUNK)

    def rows_at(owner):
        return pl.ds(pl.multiple_of(owner * rows, rows), rows)

    def in_copy(k, d):
        peer = lax.rem(band + d, nband)
        return pltpu.make_async_remote_copy(
            src_ref=x_ref.at[:, wide_at(peer, k)],
            dst_ref=xs.at[rows_at(band), cols_at(k)],
            send_sem=in_send.at[k, d - 1], recv_sem=in_recv.at[k, d - 1],
            device_id={"band": peer}, device_id_type=MESH)

    @pl.loop(0, chunks)
    def _(k):
        for d in range(1, nband):
            in_copy(k, d).start()

    local = pltpu.make_async_copy(
        x_ref.at[:, pl.ds(pl.multiple_of(band * own, own), own)], xs.at[rows_at(band)], own_sem)
    local.start()

    red[...] = jnp.zeros_like(red)
    first_tile = ((comp * nsub + sub) * nband + band) * (own // TILE)

    @pl.loop(0, own // TILE)
    def _(t):
        dense = jnp.zeros((nproj, TILE), jnp.float32)
        for b in range(nblk):
            hit = blk_ref[:, b:b + 1] == first_tile + t
            dense = dense + jnp.where(hit, proj_ref[:, b * TILE:(b + 1) * TILE], 0.0)
        at = pl.ds(pl.multiple_of(t * TILE, TILE), TILE)
        high, low = split(dense)
        y_hi[norb:, at] = high
        y_lo[norb:, at] = low

    local.wait()

    @pl.loop(0, chunks)
    def _(k):
        for d in range(1, nband):
            in_copy(k, d).wait_recv()
        at = cols_at(k)
        x = xs[:, at]
        xd = split(x)
        y_hi[:norb, at] = xd[0]
        y_lo[:norb, at] = xd[1]
        wd = split(x * v_ref[:, wide_at(band, k)])
        for base, right in ((0, xd), (pairs, wd)):
            for j0 in range(0, tri, 2):
                j1 = min(j0 + 2, tri)
                left = (xd[0][:j1 * TILE], xd[1][:j1 * TILE])
                some = (right[0][j0 * TILE:j1 * TILE], right[1][j0 * TILE:j1 * TILE])
                part = dot3(left, some, 1)
                for j in range(j0, j1):
                    for i in range(j + 1):
                        here = (base + pair_index(i, j)) * TILE
                        red[here:here + TILE] += part[
                            i * TILE:(i + 1) * TILE, (j - j0) * TILE:(j - j0 + 1) * TILE]
        part = dot3(xd, (y_hi[norb:, at], y_lo[norb:, at]), 1)
        red[2 * pairs * TILE:2 * pairs * TILE + norb] += part

    def slab(start, size):
        return pl.ds(pl.multiple_of(start, 8), size)

    low, size = 0, red.shape[0]
    stages = []
    count_before = 0
    for name, box in (("sub", sub_box), ("comp", comp_box), ("band", band_box)):
        count, me = axes[name]
        piece = size // count
        copies = []
        for d in range(1, count):
            peer = lax.rem(me + d, count)
            at = count_before + d - 1
            copies.append(pltpu.make_async_remote_copy(
                src_ref=red.at[slab(low + peer * piece, piece)], dst_ref=box.at[d - 1],
                send_sem=rs_send.at[at], recv_sem=rs_recv.at[at],
                device_id={name: peer}, device_id_type=MESH))
        for copy in copies:
            copy.start()
        mine = low + me * piece
        for d, copy in enumerate(copies):
            copy.wait_recv()
            red[slab(mine, piece)] += box[d]
        for copy in copies:
            copy.wait_send()
        low, size = mine, piece
        stages.append((name, low, size, count_before))
        count_before += count - 1

    fin[slab(low, size)] = red[slab(low, size)]
    for name, start, length, before in reversed(stages):
        count, me = axes[name]
        copies = []
        for d in range(1, count):
            copies.append(pltpu.make_async_remote_copy(
                src_ref=fin.at[slab(start, length)], dst_ref=fin.at[slab(start, length)],
                send_sem=ag_send.at[before + d - 1], recv_sem=ag_recv.at[before + d - 1],
                device_id={name: lax.rem(me + d, count)}, device_id_type=MESH))
        for copy in copies:
            copy.start()
        for copy in copies:
            copy.wait()

    coupling = fin[2 * pairs * TILE:2 * pairs * TILE + norb] * norm
    strong = coupling * en_ref[...]
    strong_d = split(strong)
    coupling_d = split(coupling)
    last = split(strong * (-step_size * norm))
    lm_hi[:, norb:] = last[0]
    lm_lo[:, norb:] = last[1]
    for j in range(tri):
        js = slice(j * TILE, (j + 1) * TILE)
        nonlocal_part = dot3(
            (strong_d[0][:(j + 1) * TILE], strong_d[1][:(j + 1) * TILE]),
            (coupling_d[0][js], coupling_d[1][js]), 1)
        for i in range(j + 1):
            is_ = slice(i * TILE, (i + 1) * TILE)
            here = pair_index(i, j) * TILE
            corr = fin[here:here + TILE] * (-0.5 / total_coef)
            here = (pairs + pair_index(i, j)) * TILE
            lag = (fin[here:here + TILE] + nonlocal_part[is_]) * (step_size / total_coef)
            for value, hi_ref, lo_ref in ((corr, om_hi, om_lo), (lag, lm_hi, lm_lo)):
                hi, lo = split(value)
                hi_ref[is_, js] = hi
                lo_ref[is_, js] = lo
                if i != j:
                    hi, lo = split(value.T)
                    hi_ref[js, is_] = hi
                    lo_ref[js, is_] = lo

    def out_copy(k, d):
        peer = lax.rem(band + d, nband)
        return pltpu.make_async_remote_copy(
            src_ref=res.at[rows_at(peer), cols_at(k)],
            dst_ref=out_ref.at[:, wide_at(band, k)],
            send_sem=out_send.at[k, d - 1], recv_sem=out_recv.at[k, d - 1],
            device_id={"band": peer}, device_id_type=MESH)

    def keep_copy(k):
        return pltpu.make_async_copy(
            res.at[rows_at(band), cols_at(k)], out_ref.at[:, wide_at(band, k)], keep_sem.at[k])

    @pl.loop(0, chunks)
    def _(k):
        at = cols_at(k)
        x = xs[:, at]
        z = x - step_size * (x * v_ref[:, wide_at(band, k)])
        z = z + dot3((lm_hi[...], lm_lo[...]), (y_hi[:, at], y_lo[:, at]), 0)
        res[:, at] = 1.5 * z + dot3((om_hi[...], om_lo[...]), split(z), 0)
        for d in range(1, nband):
            out_copy(k, d).start()
        keep_copy(k).start()

    @pl.loop(0, chunks)
    def _(k):
        for d in range(1, nband):
            in_copy(k, d).wait_send()
            out_copy(k, d).wait()
        keep_copy(k).wait()


def on_device(orbitals, potential, proj_values, block_list, proj_energy):
    nband, ncomp, nsub = (lax.axis_size(name) for name in ("band", "comp", "sub"))
    atom_count, proj_count, proj_len = proj_values.shape
    nproj = atom_count * proj_count
    rows, row_width = orbitals.shape
    norb, own = rows * nband, row_width // nband
    chunks = own // CHUNK
    proj = proj_values.reshape(nproj, proj_len)
    blocks = jnp.repeat(block_list, proj_count, axis=0)
    energy = proj_energy.reshape(1, nproj)
    tri = norb // TILE
    need = tri * (tri + 1) * TILE + norb
    unit = 8 * nband * ncomp * nsub
    full = -(-need // unit) * unit
    f32, bf16, dma = jnp.float32, jnp.bfloat16, pltpu.SemaphoreType.DMA
    hops = nband + ncomp + nsub - 3
    half, quarter = full // nsub, full // (nsub * ncomp)
    vmem = pl.BlockSpec(memory_space=pltpu.VMEM)
    return pl.pallas_call(
        functools.partial(step_kernel, (nband, ncomp, nsub)),
        out_shape=jax.ShapeDtypeStruct(orbitals.shape, f32),
        in_specs=[pl.BlockSpec(memory_space=pl.ANY), vmem, vmem, vmem, vmem],
        out_specs=pl.BlockSpec(memory_space=pl.ANY),
        scratch_shapes=[
            pltpu.VMEM((norb, own), f32),
            pltpu.VMEM((norb + nproj, own), bf16),
            pltpu.VMEM((norb + nproj, own), bf16),
            pltpu.VMEM((full, TILE), f32),
            pltpu.VMEM((full, TILE), f32),
            pltpu.VMEM((norb, norb + nproj), bf16),
            pltpu.VMEM((norb, norb + nproj), bf16),
            pltpu.VMEM((norb, norb), bf16),
            pltpu.VMEM((norb, norb), bf16),
            pltpu.VMEM((norb, own), f32),
            pltpu.VMEM((nsub - 1, half, TILE), f32),
            pltpu.VMEM((ncomp - 1, quarter, TILE), f32),
            pltpu.VMEM((nband - 1, quarter // nband, TILE), f32),
            dma,
            dma((chunks, nband - 1)), dma((chunks, nband - 1)),
            dma((chunks, nband - 1)), dma((chunks, nband - 1)),
            dma((chunks,)),
            dma((hops,)), dma((hops,)), dma((hops,)), dma((hops,)),
        ],
        compiler_params=pltpu.CompilerParams(
            collective_id=0, has_side_effects=True, vmem_limit_bytes=48 * 1024 * 1024),
    )(orbitals, potential.reshape(1, row_width), proj, blocks, energy)


def solution(mesh):
    in_specs = (
        P(("groups", "band"), ("comp", "sub")),
        P(("groups", "comp", "sub")),
        P("groups", None, None),
        P("groups", None),
        P("groups", None),
    )
    out_specs = P(("groups", "band"), ("comp", "sub"))
    return jax.shard_map(
        on_device, mesh=mesh, in_specs=in_specs, out_specs=out_specs, check_vma=False
    )
```

time: 364 us -> 150 us (0.41); the launches traced: 360 us -> 150 us
  waiting for transfers between devices: 168 us -> 0 us
  Pallas kernels: 0 us -> 143 us
  matrix products: 59.8 us -> 0 us
  blocking collectives: 49.1 us -> 0 us
  other arithmetic: 35.7 us -> 0 us
  local copies, waits for them, and re-layouts: 22.7 us -> 6.49 us
  between operations: 13.5 us -> 0.03 us
  starting transfers between devices: 10.6 us -> 0 us
    pallas_call x0 -> x1, Pallas kernels: none -> 143 us  [on_device(): pl.pallas_call(functools.partial(step_kernel, (nband, ncomp, nsub)), out_...]
    psum x2 -> x0, waiting for transfers between devices: 130 us -> none  [the longest x1 99.6 us: on_device(): correlation, hmat = lax.psum((correlation, h_part), ('band', 'comp', 'sub'))]
    dot_general x7 -> x0, matrix products: 59.8 us -> none  [the longest x1 18.6 us: on_device(): jnp.einsum('akbc,aki->iabc', weighted, coupling, precision=highest)]
    all_to_all x1 -> x0, blocking collectives: 49.1 us -> none  [on_device(): lax.all_to_all(result, 'band', split_axis=0, concat_axis=1, tiled=True)]
    all_to_all x2 -> x0, waiting for transfers between devices: 37.8 us -> none  [the longest x1 37.8 us: on_device(): lax.all_to_all(hpsi, 'band', split_axis=1, concat_axis=0, tiled=True)]
    scatter-add x1 -> x0, other arithmetic: 33.1 us -> none  [on_device(): extra = jnp.zeros_like(tiles).at[:, safe_idx].add(contrib)]
    all_to_all x2 -> x0, starting transfers between devices: 10.6 us -> none  [the longest x1 5.45 us: on_device(): lax.all_to_all(orbitals, 'band', split_axis=1, concat_axis=0, tiled=True)]
    gather x1 -> x0, local copies, waits for them, and re-layouts: 7.37 us -> none  [on_device(): picked = tiles[:, safe_idx] * inside[None, :, :, None]]
  transfers between devices with their start and end apart: 4 -> 0, of which waited for: 3 -> 0; matrix products, arithmetic and copies ran while one was open for 26% -> 0% of each run, Pallas kernels for 0% -> 0%
where the time goes in v1:
time: 150 us
  Pallas kernels  143 us (95%)
  local copies, waits for them, and re-layouts  6.49 us (4%)
    pallas_call x1, Pallas kernels, on_device(): pl.pallas_call(functools.partial(step_kernel, (nband, ncomp, nsub)), out_...  143 us
    unnamed x7, local copies, waits for them, and re-layouts  5.15 us

profile of v1, /device:TPU:14, one launch (start us, length us, event | category | flops | bytes accessed | tf_op | source)
XLA Modules:
  0.0 149.5 jit_solution(13654203314959087922)
XLA Ops:
  0.0 0.8 copy.8
  0.8 0.8 copy.9
  1.5 0.1 reshape.15.en_ref
  1.7 1.2 reshape.13.proj_ref
  2.9 0.0 copy-start
  2.9 1.6 %copy-done = f32[128,4096]{1,0:T(8,128)S(1)} copy-done((f32[128,4096]{1,0:T(8,128)S(1)}, f32[128,4096]{1,0:T(8,128)}, u32[]{:S(2)}) %copy-start) | copy-done | bytes 2097176
  4.5 0.0 copy-start.1
  4.5 0.7 copy-done.1
  5.2 143.0 %shard_map.55 = f32[128,4096]{1,0:T(8,128)S(1)} custom-call(f32[128,4096]{1,0:T(8,128)S(1)} %copy-done, f32[1,4096]{1,0:T(1,128)S(1)} %bitcast.3, f32[128,1024]{1,0:T(8,128)S(1)} %reshape.13.proj_ref, s32[128,8]{1,0:T(8,128)S(1)} %bitcast.2, f32[1,128]{1,0:T(1,128)S(1)} %reshape.15.en_ref), custom_call_target="tpu_custom_call" | custom-call | tf_op jit(solution)/shard_map/pallas_call | solution.py:247
  148.2 1.3 copy.11
  (1 shorter events, 0.0 us)
Async XLA Ops:
  2.9 1.6 %copy-start = (f32[128,4096]{1,0:T(8,128)S(1)}, f32[128,4096]{1,0:T(8,128)}, u32[]{:S(2)}) copy-start(f32[128,4096]{1,0:T(8,128)} %x_ref.1) | copy-start | bytes 6291460
  4.5 0.7 copy-start.1

commit v2 on v1

--- a/solution.py
+++ b/solution.py
@@ -28,23 +28,25 @@
     return one(a[0], b[0]) + (one(a[0], b[1]) + one(a[1], b[0]))
 
 
-def pair_index(i, j):
-    return j * (j + 1) // 2 + i
+def pair_index(i, j, early):
+    return j * (j - 1) // 2 + i if early else j * (j + 1) // 2 + i
 
 
 def step_kernel(sizes, x_ref, v_ref, proj_ref, blk_ref, en_ref, out_ref,
                 xs, y_hi, y_lo, red, fin, lm_hi, lm_lo, om_hi, om_lo, res,
                 sub_box, comp_box, band_box, own_sem,
                 in_send, in_recv, out_send, out_recv, keep_sem,
-                rs_send, rs_recv, ag_send, ag_recv):
+                sub_send, sub_recv, comp_send, comp_recv, band_send, band_recv,
+                proj_buf, proj_sem, *more):
     nband, ncomp, nsub = sizes
     rows = x_ref.shape[0]
     norb, own = xs.shape
     nproj = proj_ref.shape[0]
+    early = bool(more)
     nblk = blk_ref.shape[1]
     chunks = own // CHUNK
     tri = norb // TILE
-    pairs = tri * (tri + 1) // 2
+    pairs = tri * (tri - 1) // 2 if early else tri * (tri + 1) // 2
     total_coef = own * nband * ncomp * nsub
     norm = 1.0 / math.sqrt(nblk * TILE)
     band = lax.axis_index("band")
@@ -84,20 +86,87 @@
     local = pltpu.make_async_copy(
         x_ref.at[:, pl.ds(pl.multiple_of(band * own, own), own)], xs.at[rows_at(band)], own_sem)
     local.start()
-
+    get_proj = pltpu.make_async_copy(proj_ref, proj_buf, proj_sem)
+    get_proj.start()
+    if early:
+        (x_own, p_hi, p_lo, part, sums, half_box, quarter_box, x_sem,
+         e_send, e_recv, f_send, f_recv) = more
+        get_x = pltpu.make_async_copy(x_ref, x_own, x_sem)
+        get_x.start()
     red[...] = jnp.zeros_like(red)
-    first_tile = ((comp * nsub + sub) * nband + band) * (own // TILE)
-
-    @pl.loop(0, own // TILE)
-    def _(t):
+    get_proj.wait()
+
+    def dense_tile(tile):
         dense = jnp.zeros((nproj, TILE), jnp.float32)
         for b in range(nblk):
-            hit = blk_ref[:, b:b + 1] == first_tile + t
-            dense = dense + jnp.where(hit, proj_ref[:, b * TILE:(b + 1) * TILE], 0.0)
-        at = pl.ds(pl.multiple_of(t * TILE, TILE), TILE)
-        high, low = split(dense)
-        y_hi[norb:, at] = high
-        y_lo[norb:, at] = low
+            hit = blk_ref[:, b:b + 1] == tile
+            dense = dense + jnp.where(hit, proj_buf[:, b * TILE:(b + 1) * TILE], 0.0)
+        return split(dense)
+
+    here_first = (comp * nsub + sub) * nband * (own // TILE)
+    if early:
+        part[...] = jnp.zeros_like(part)
+        get_x.wait()
+
+        @pl.loop(0, nband * own // CHUNK)
+        def _(k):
+            tiles = [dense_tile(here_first + k * (CHUNK // TILE) + t)
+                     for t in range(CHUNK // TILE)]
+            p_d = tuple(jnp.concatenate([t[h] for t in tiles], axis=1) for h in range(2))
+            at = cols_at(k)
+            p_hi[:, at] = p_d[0]
+            p_lo[:, at] = p_d[1]
+            x = x_own[:, at]
+            x_d = split(x)
+            part[:TILE] += dot3(x_d, x_d, 1)
+            part[TILE:2 * TILE] += dot3(x_d, split(x * v_ref[:, at]), 1)
+            part[2 * TILE:] += dot3(x_d, p_d, 1)
+
+        mine_cols = pl.ds(pl.multiple_of(band * own, own), own)
+        y_hi[norb:] = p_hi[:, mine_cols]
+        y_lo[norb:] = p_lo[:, mine_cols]
+    else:
+        @pl.loop(0, own // TILE)
+        def _(t):
+            at = pl.ds(pl.multiple_of(t * TILE, TILE), TILE)
+            high, low = dense_tile(here_first + band * (own // TILE) + t)
+            y_hi[norb:, at] = high
+            y_lo[norb:, at] = low
+
+    def slab(start, size):
+        return pl.ds(pl.multiple_of(start, 8), size)
+
+    def remote(src, dst, send, recv, name, d):
+        count, me = axes[name]
+        return pltpu.make_async_remote_copy(
+            src_ref=src, dst_ref=dst, send_sem=send, recv_sem=recv,
+            device_id={name: lax.rem(me + d, count)}, device_id_type=MESH)
+
+    if early:
+        e_low, e_size, before = 0, 3 * TILE, 0
+        for name, box in (("sub", half_box), ("comp", quarter_box)):
+            count, me = axes[name]
+            e_size //= count
+            copies = [
+                remote(part.at[slab(e_low + lax.rem(me + d, count) * e_size, e_size)],
+                       box.at[d - 1], e_send.at[before + d - 1], e_recv.at[before + d - 1],
+                       name, d)
+                for d in range(1, count)]
+            for copy in copies:
+                copy.start()
+            e_low = e_low + me * e_size
+            for d, copy in enumerate(copies):
+                copy.wait_recv()
+                part[slab(e_low, e_size)] += box[d]
+            for copy in copies:
+                copy.wait_send()
+            before += count - 1
+        sums[band, slab(e_low, e_size)] = part[slab(e_low, e_size)]
+        mine = sums.at[band, slab(e_low, e_size)]
+        e_band = [remote(mine, mine, f_send.at[d - 1], f_recv.at[d - 1], "band", d)
+                  for d in range(1, nband)]
+        for copy in e_band:
+            copy.start()
 
     local.wait()
 
@@ -114,61 +183,119 @@
         for base, right in ((0, xd), (pairs, wd)):
             for j0 in range(0, tri, 2):
                 j1 = min(j0 + 2, tri)
-                left = (xd[0][:j1 * TILE], xd[1][:j1 * TILE])
+                j0 = max(j0, 1) if early else j0
+                reach = (j1 - 1 if early else j1) * TILE
+                left = (xd[0][:reach], xd[1][:reach])
                 some = (right[0][j0 * TILE:j1 * TILE], right[1][j0 * TILE:j1 * TILE])
-                part = dot3(left, some, 1)
+                got = dot3(left, some, 1)
                 for j in range(j0, j1):
-                    for i in range(j + 1):
-                        here = (base + pair_index(i, j)) * TILE
-                        red[here:here + TILE] += part[
+                    for i in range(j if early else j + 1):
+                        here = (base + pair_index(i, j, early)) * TILE
+                        red[here:here + TILE] += got[
                             i * TILE:(i + 1) * TILE, (j - j0) * TILE:(j - j0 + 1) * TILE]
-        part = dot3(xd, (y_hi[norb:, at], y_lo[norb:, at]), 1)
-        red[2 * pairs * TILE:2 * pairs * TILE + norb] += part
-
-    def slab(start, size):
-        return pl.ds(pl.multiple_of(start, 8), size)
-
-    low, size = 0, red.shape[0]
-    stages = []
-    count_before = 0
-    for name, box in (("sub", sub_box), ("comp", comp_box), ("band", band_box)):
-        count, me = axes[name]
-        piece = size // count
-        copies = []
-        for d in range(1, count):
-            peer = lax.rem(me + d, count)
-            at = count_before + d - 1
-            copies.append(pltpu.make_async_remote_copy(
-                src_ref=red.at[slab(low + peer * piece, piece)], dst_ref=box.at[d - 1],
-                send_sem=rs_send.at[at], recv_sem=rs_recv.at[at],
-                device_id={name: peer}, device_id_type=MESH))
+        if not early:
+            red[2 * pairs * TILE:2 * pairs * TILE + norb] += dot3(
+                xd, (y_hi[norb:, at], y_lo[norb:, at]), 1)
+
+    half = red.shape[0] // nsub
+    quarter = half // ncomp
+    unit = quarter // nband
+    half_low = sub * half
+    low = half_low + comp * quarter
+    own_low = low + band * unit
+
+    to_sub = [remote(red.at[slab(lax.rem(sub + d, nsub) * half, half)], sub_box.at[d - 1],
+                     sub_send.at[0, d - 1], sub_recv.at[0, d - 1], "sub", d)
+              for d in range(1, nsub)]
+    for copy in to_sub:
+        copy.start()
+    for d, copy in enumerate(to_sub):
+        copy.wait_recv()
+        red[slab(half_low, half)] += sub_box[d]
+
+    to_comp = [[remote(red.at[slab(half_low + lax.rem(comp + d, ncomp) * quarter
+                                   + lax.rem(band + q, nband) * unit, unit)],
+                       comp_box.at[d - 1, lax.rem(band + q, nband)],
+                       comp_send.at[0, d - 1, lax.rem(band + q, nband)],
+                       comp_recv.at[0, d - 1, lax.rem(band + q, nband)], "comp", d)
+                for d in range(1, ncomp)] for q in range(1, nband + 1)]
+    for copies in to_comp:
         for copy in copies:
             copy.start()
-        mine = low + me * piece
-        for d, copy in enumerate(copies):
+    to_band = []
+    for q in range(1, nband + 1):
+        owner = lax.rem(band + q, nband)
+        piece = slab(low + owner * unit, unit)
+        for d, copy in enumerate(to_comp[q - 1]):
             copy.wait_recv()
-            red[slab(mine, piece)] += box[d]
-        for copy in copies:
-            copy.wait_send()
-        low, size = mine, piece
-        stages.append((name, low, size, count_before))
-        count_before += count - 1
-
-    fin[slab(low, size)] = red[slab(low, size)]
-    for name, start, length, before in reversed(stages):
-        count, me = axes[name]
-        copies = []
-        for d in range(1, count):
-            copies.append(pltpu.make_async_remote_copy(
-                src_ref=fin.at[slab(start, length)], dst_ref=fin.at[slab(start, length)],
-                send_sem=ag_send.at[before + d - 1], recv_sem=ag_recv.at[before + d - 1],
-                device_id={name: lax.rem(me + d, count)}, device_id_type=MESH))
-        for copy in copies:
-            copy.start()
-        for copy in copies:
-            copy.wait()
-
-    coupling = fin[2 * pairs * TILE:2 * pairs * TILE + norb] * norm
+            red[piece] += comp_box[d, owner]
+        if q < nband:
+            copy = remote(red.at[piece], band_box.at[q - 1],
+                          band_send.at[0, q - 1], band_recv.at[0, q - 1], "band", q)
+            copy.start()
+            to_band.append(copy)
+    if early:
+        for copy in e_band:
+            copy.wait_recv()
+        every = sums.at[:, slab(e_low, e_size)]
+        e_comp = [remote(every, every, e_send.at[before + d - 1], e_recv.at[before + d - 1],
+                         "comp", d) for d in range(1, ncomp)]
+        for copy in e_comp:
+            copy.start()
+    for d, copy in enumerate(to_band):
+        copy.wait_recv()
+        red[slab(own_low, unit)] += band_box[d]
+
+    fin[slab(own_low, unit)] = red[slab(own_low, unit)]
+    mine = fin.at[slab(own_low, unit)]
+    back_band = [remote(mine, mine, band_send.at[1, d - 1], band_recv.at[1, d - 1], "band", d)
+                 for d in range(1, nband)]
+    for copy in back_band:
+        copy.start()
+    back_comp = []
+    for q in range(nband):
+        if q:
+            back_band[q - 1].wait_recv()
+        owner = lax.rem(band + nband - q, nband)
+        piece = fin.at[slab(low + owner * unit, unit)]
+        for d in range(1, ncomp):
+            copy = remote(piece, piece, comp_send.at[1, d - 1, q], comp_recv.at[1, d - 1, q],
+                          "comp", d)
+            copy.start()
+            back_comp.append(copy)
+    if early:
+        for copy in e_comp:
+            copy.wait_recv()
+        e_half = e_low - comp * e_size
+        every = sums.at[:, slab(e_half, ncomp * e_size)]
+        e_sub = [remote(every, every, e_send.at[before + ncomp - 1 + d - 1],
+                        e_recv.at[before + ncomp - 1 + d - 1], "sub", d)
+                 for d in range(1, nsub)]
+        for copy in e_sub:
+            copy.start()
+    for copy in back_comp:
+        copy.wait_recv()
+    mine = fin.at[slab(half_low, half)]
+    back_sub = [remote(mine, mine, sub_send.at[1, d - 1], sub_recv.at[1, d - 1], "sub", d)
+                for d in range(1, nsub)]
+    for copy in back_sub:
+        copy.start()
+    if early:
+        for copy in e_sub:
+            copy.wait_recv()
+    for copy in back_sub:
+        copy.wait_recv()
+
+    def summed(kind, i, j):
+        if early and i == j:
+            return sums[i, kind * TILE:(kind + 1) * TILE]
+        here = (kind * pairs + pair_index(i, j, early)) * TILE
+        return fin[here:here + TILE]
+
+    if early:
+        coupling = jnp.concatenate([sums[i, 2 * TILE:] for i in range(tri)], axis=0) * norm
+    else:
+        coupling = fin[2 * pairs * TILE:2 * pairs * TILE + norb] * norm
     strong = coupling * en_ref[...]
     strong_d = split(strong)
     coupling_d = split(coupling)
@@ -182,10 +309,8 @@
             (coupling_d[0][js], coupling_d[1][js]), 1)
         for i in range(j + 1):
             is_ = slice(i * TILE, (i + 1) * TILE)
-            here = pair_index(i, j) * TILE
-            corr = fin[here:here + TILE] * (-0.5 / total_coef)
-            here = (pairs + pair_index(i, j)) * TILE
-            lag = (fin[here:here + TILE] + nonlocal_part[is_]) * (step_size / total_coef)
+            corr = summed(0, i, j) * (-0.5 / total_coef)
+            lag = (summed(1, i, j) + nonlocal_part[is_]) * (step_size / total_coef)
             for value, hi_ref, lo_ref in ((corr, om_hi, om_lo), (lag, lm_hi, lm_lo)):
                 hi, lo = split(value)
                 hi_ref[is_, js] = hi
@@ -224,6 +349,14 @@
             in_copy(k, d).wait_send()
             out_copy(k, d).wait()
         keep_copy(k).wait()
+
+    sent = to_sub + to_band + back_band + back_comp + back_sub
+    for copies in to_comp:
+        sent = sent + copies
+    if early:
+        sent = sent + e_band + e_comp + e_sub
+    for copy in sent:
+        copy.wait_send()
 
 
 def on_device(orbitals, potential, proj_values, block_list, proj_energy):
@@ -237,18 +370,34 @@
     blocks = jnp.repeat(block_list, proj_count, axis=0)
     energy = proj_energy.reshape(1, nproj)
     tri = norb // TILE
-    need = tri * (tri + 1) * TILE + norb
+    early = rows == TILE and nproj == TILE and 3 * TILE % (8 * ncomp * nsub) == 0
+    need = tri * (tri - 1) * TILE if early else tri * (tri + 1) * TILE + norb
     unit = 8 * nband * ncomp * nsub
     full = -(-need // unit) * unit
     f32, bf16, dma = jnp.float32, jnp.bfloat16, pltpu.SemaphoreType.DMA
-    hops = nband + ncomp + nsub - 3
+    more = []
+    if early:
+        hops = 2 * (nsub + ncomp - 2)
+        e_half = 3 * TILE // nsub
+        more = [
+            pltpu.VMEM((rows, row_width), f32),
+            pltpu.VMEM((nproj, row_width), bf16),
+            pltpu.VMEM((nproj, row_width), bf16),
+            pltpu.VMEM((3 * TILE, TILE), f32),
+            pltpu.VMEM((nband, 3 * TILE, TILE), f32),
+            pltpu.VMEM((nsub - 1, e_half, TILE), f32),
+            pltpu.VMEM((ncomp - 1, e_half // ncomp, TILE), f32),
+            dma,
+            dma((hops,)), dma((hops,)), dma((nband - 1,)), dma((nband - 1,)),
+        ]
     half, quarter = full // nsub, full // (nsub * ncomp)
+    anywhere = pl.BlockSpec(memory_space=pl.ANY)
     vmem = pl.BlockSpec(memory_space=pltpu.VMEM)
     return pl.pallas_call(
         functools.partial(step_kernel, (nband, ncomp, nsub)),
         out_shape=jax.ShapeDtypeStruct(orbitals.shape, f32),
-        in_specs=[pl.BlockSpec(memory_space=pl.ANY), vmem, vmem, vmem, vmem],
-        out_specs=pl.BlockSpec(memory_space=pl.ANY),
+        in_specs=[anywhere, vmem, anywhere, vmem, vmem],
+        out_specs=anywhere,
         scratch_shapes=[
             pltpu.VMEM((norb, own), f32),
             pltpu.VMEM((norb + nproj, own), bf16),
@@ -261,13 +410,17 @@
             pltpu.VMEM((norb, norb), bf16),
             pltpu.VMEM((norb, own), f32),
             pltpu.VMEM((nsub - 1, half, TILE), f32),
-            pltpu.VMEM((ncomp - 1, quarter, TILE), f32),
+            pltpu.VMEM((ncomp - 1, nband, quarter // nband, TILE), f32),
             pltpu.VMEM((nband - 1, quarter // nband, TILE), f32),
             dma,
             dma((chunks, nband - 1)), dma((chunks, nband - 1)),
             dma((chunks, nband - 1)), dma((chunks, nband - 1)),
             dma((chunks,)),
-            dma((hops,)), dma((hops,)), dma((hops,)), dma((hops,)),
+            dma((2, nsub - 1)), dma((2, nsub - 1)),
+            dma((2, ncomp - 1, nband)), dma((2, ncomp - 1, nband)),
+            dma((2, nband - 1)), dma((2, nband - 1)),
+            pltpu.VMEM((nproj, proj_len), f32), dma,
+            *more,
         ],
         compiler_params=pltpu.CompilerParams(
             collective_id=0, has_side_effects=True, vmem_limit_bytes=48 * 1024 * 1024),

time: 150 us -> 130 us (0.87); the launches traced: 150 us -> 127 us
  Pallas kernels: 143 us -> 121 us
    pallas_call x1, Pallas kernels: 143 us -> 121 us  [on_device(): pl.pallas_call(functools.partial(step_kernel, (nband, ncomp, nsub)), out_...]
where the time goes in v2:
time: 130 us; the launch traced here: 127 us
  Pallas kernels  121 us (93%)
  local copies, waits for them, and re-layouts  6.49 us (5%)
    pallas_call x1, Pallas kernels, on_device(): pl.pallas_call(functools.partial(step_kernel, (nband, ncomp, nsub)), out_...  121 us
    unnamed x7, local copies, waits for them, and re-layouts  5.15 us

profile of v2, /device:TPU:14, one launch (start us, length us, event | category | flops | bytes accessed | tf_op | source)
XLA Modules:
  0.0 127.3 jit_solution(7232458770115910370)
XLA Ops:
  0.0 0.8 copy.8
  0.8 0.8 copy.9
  1.5 0.1 reshape.15.en_ref
  1.7 1.2 reshape.13.proj_ref
  2.9 0.0 copy-start
  2.9 1.6 %copy-done = f32[128,4096]{1,0:T(8,128)S(1)} copy-done((f32[128,4096]{1,0:T(8,128)S(1)}, f32[128,4096]{1,0:T(8,128)}, u32[]{:S(2)}) %copy-start) | copy-done | bytes 2097176
  4.5 0.0 copy-start.1
  4.5 0.7 copy-done.1
  5.2 120.8 %shard_map.55 = f32[128,4096]{1,0:T(8,128)S(1)} custom-call(f32[128,4096]{1,0:T(8,128)S(1)} %copy-done, f32[1,4096]{1,0:T(1,128)S(1)} %bitcast.3, f32[128,1024]{1,0:T(8,128)S(1)} %reshape.13.proj_ref, s32[128,8]{1,0:T(8,128)S(1)} %bitcast.2, f32[1,128]{1,0:T(1,128)S(1)} %reshape.15.en_ref), custom_call_target="tpu_custom_call" | custom-call | tf_op jit(solution)/shard_map/pallas_call | solution.py:396
  126.0 1.3 %copy.11 = f32[128,4096]{1,0:T(8,128)} copy(f32[128,4096]{1,0:T(8,128)S(1)} %shard_map.55) | data formatting | bytes 4194304
  (1 shorter events, 0.0 us)
Async XLA Ops:
  2.9 1.6 %copy-start = (f32[128,4096]{1,0:T(8,128)S(1)}, f32[128,4096]{1,0:T(8,128)}, u32[]{:S(2)}) copy-start(f32[128,4096]{1,0:T(8,128)} %x_ref.1) | copy-start | bytes 6291460
  4.5 0.7 copy-start.1

commit v3 on v2

--- a/solution.py
+++ b/solution.py
@@ -90,7 +90,8 @@
     get_proj.start()
     if early:
         (x_own, p_hi, p_lo, part, sums, half_box, quarter_box, x_sem,
-         e_send, e_recv, f_send, f_recv) = more
+         e_send, e_recv, f_send, f_recv,
+         xe, ze, rese, xe_send, xe_recv, side_send, side_recv, side_sem) = more
         get_x = pltpu.make_async_copy(x_ref, x_own, x_sem)
         get_x.start()
     red[...] = jnp.zeros_like(red)
@@ -107,6 +108,20 @@
     if early:
         part[...] = jnp.zeros_like(part)
         get_x.wait()
+        group = nband // 2
+        first = band // group * group
+        far = lax.rem(band + group, nband)
+        xe[rows_at(band)] = x_own[:, wide_at(far, chunks - 1)]
+        xe_copies = []
+        for d in range(1, nband):
+            to = lax.rem(band + d, nband)
+            xe_copies.append(pltpu.make_async_remote_copy(
+                src_ref=x_ref.at[:, wide_at(lax.rem(to + group, nband), chunks - 1)],
+                dst_ref=xe.at[rows_at(band)],
+                send_sem=xe_send.at[d - 1], recv_sem=xe_recv.at[d - 1],
+                device_id={"band": to}, device_id_type=MESH))
+        for copy in xe_copies:
+            copy.start()
 
         @pl.loop(0, nband * own // CHUNK)
         def _(k):
@@ -332,29 +347,77 @@
         return pltpu.make_async_copy(
             res.at[rows_at(band), cols_at(k)], out_ref.at[:, wide_at(band, k)], keep_sem.at[k])
 
-    @pl.loop(0, chunks)
-    def _(k):
+    def mixed(k):
         at = cols_at(k)
         x = xs[:, at]
         z = x - step_size * (x * v_ref[:, wide_at(band, k)])
         z = z + dot3((lm_hi[...], lm_lo[...]), (y_hi[:, at], y_lo[:, at]), 0)
         res[:, at] = 1.5 * z + dot3((om_hi[...], om_lo[...]), split(z), 0)
+        keep_copy(k).start()
+
+    over = chunks - 1 if early else chunks
+
+    @pl.loop(0, over)
+    def _(k):
+        mixed(k)
         for d in range(1, nband):
             out_copy(k, d).start()
-        keep_copy(k).start()
+
+    if early:
+        def side_copy(slot, d, src, owner):
+            peer = lax.rem(band - first + d, group)
+            return pltpu.make_async_remote_copy(
+                src_ref=src(peer), dst_ref=out_ref.at[:, wide_at(owner, over)],
+                send_sem=side_send.at[slot, d - 1], recv_sem=side_recv.at[slot, d - 1],
+                device_id={"band": first + peer}, device_id_type=MESH)
+
+        mixed(over)
+        near_copies = [
+            side_copy(0, d, lambda peer: res.at[rows_at(first + peer), cols_at(over)], band)
+            for d in range(1, group)]
+        for copy in near_copies:
+            copy.start()
+        for copy in xe_copies:
+            copy.wait_recv()
+        x = xe[...]
+        x_d = split(x)
+        far_cols = wide_at(far, over)
+        z = x - step_size * (x * v_ref[:, far_cols])
+        both = (jnp.concatenate([x_d[0], p_hi[:, far_cols]], axis=0),
+                jnp.concatenate([x_d[1], p_lo[:, far_cols]], axis=0))
+        z = z + dot3((lm_hi[...], lm_lo[...]), both, 0)
+        ze[...] = z
+        some = pl.ds(pl.multiple_of(first * rows, rows), group * rows)
+        rese[...] = 1.5 * ze[some] + dot3((om_hi[some], om_lo[some]), split(z), 0)
+        far_copies = [side_copy(1, d, lambda peer: rese.at[rows_at(peer)], far)
+                      for d in range(1, group)]
+        for copy in far_copies:
+            copy.start()
+        keep_far = pltpu.make_async_copy(
+            rese.at[rows_at(band - first)], out_ref.at[:, far_cols], side_sem)
+        keep_far.start()
 
     @pl.loop(0, chunks)
     def _(k):
         for d in range(1, nband):
             in_copy(k, d).wait_send()
+        keep_copy(k).wait()
+
+    @pl.loop(0, over)
+    def _(k):
+        for d in range(1, nband):
             out_copy(k, d).wait()
-        keep_copy(k).wait()
+
+    if early:
+        keep_far.wait()
+        for copy in near_copies + far_copies:
+            copy.wait()
 
     sent = to_sub + to_band + back_band + back_comp + back_sub
     for copies in to_comp:
         sent = sent + copies
     if early:
-        sent = sent + e_band + e_comp + e_sub
+        sent = sent + e_band + e_comp + e_sub + xe_copies
     for copy in sent:
         copy.wait_send()
 
@@ -370,7 +433,7 @@
     blocks = jnp.repeat(block_list, proj_count, axis=0)
     energy = proj_energy.reshape(1, nproj)
     tri = norb // TILE
-    early = rows == TILE and nproj == TILE and 3 * TILE % (8 * ncomp * nsub) == 0
+    early = rows == TILE and nband % 2 == 0 and nband > 2 and nproj == TILE and 3 * TILE % (8 * ncomp * nsub) == 0
     need = tri * (tri - 1) * TILE if early else tri * (tri + 1) * TILE + norb
     unit = 8 * nband * ncomp * nsub
     full = -(-need // unit) * unit
@@ -389,6 +452,11 @@
             pltpu.VMEM((ncomp - 1, e_half // ncomp, TILE), f32),
             dma,
             dma((hops,)), dma((hops,)), dma((nband - 1,)), dma((nband - 1,)),
+            pltpu.VMEM((norb, CHUNK), f32),
+            pltpu.VMEM((norb, CHUNK), f32),
+            pltpu.VMEM((norb // 2, CHUNK), f32),
+            dma((nband - 1,)), dma((nband - 1,)),
+            dma((2, nband // 2 - 1)), dma((2, nband // 2 - 1)), dma,
         ]
     half, quarter = full // nsub, full // (nsub * ncomp)
     anywhere = pl.BlockSpec(memory_space=pl.ANY)

time: 130 us -> 125 us (0.962)
  Pallas kernels: 121 us -> 117 us
    pallas_call x1, Pallas kernels: 121 us -> 117 us  [on_device(): pl.pallas_call(functools.partial(step_kernel, (nband, ncomp, nsub)), out_...]
where the time goes in v3:
time: 125 us; the launch traced here: 123 us
  Pallas kernels  117 us (94%)
  local copies, waits for them, and re-layouts  6.49 us (5%)
    pallas_call x1, Pallas kernels, on_device(): pl.pallas_call(functools.partial(step_kernel, (nband, ncomp, nsub)), out_...  117 us
    unnamed x7, local copies, waits for them, and re-layouts  5.15 us

profile of v3, /device:TPU:14, one launch (start us, length us, event | category | flops | bytes accessed | tf_op | source)
XLA Modules:
  0.0 123.0 jit_solution(1964021707076968463)
XLA Ops:
  0.0 0.8 copy.8
  0.8 0.8 copy.9
  1.5 0.1 reshape.15.en_ref
  1.7 1.2 reshape.13.proj_ref
  2.9 0.0 copy-start
  2.9 1.6 %copy-done = f32[128,4096]{1,0:T(8,128)S(1)} copy-done((f32[128,4096]{1,0:T(8,128)S(1)}, f32[128,4096]{1,0:T(8,128)}, u32[]{:S(2)}) %copy-start) | copy-done | bytes 2097176
  4.5 0.0 copy-start.1
  4.5 0.7 copy-done.1
  5.2 116.5 %shard_map.55 = f32[128,4096]{1,0:T(8,128)S(1)} custom-call(f32[128,4096]{1,0:T(8,128)S(1)} %copy-done, f32[1,4096]{1,0:T(1,128)S(1)} %bitcast.3, f32[128,1024]{1,0:T(8,128)S(1)} %reshape.13.proj_ref, s32[128,8]{1,0:T(8,128)S(1)} %bitcast.2, f32[1,128]{1,0:T(1,128)S(1)} %reshape.15.en_ref), custom_call_target="tpu_custom_call" | custom-call | tf_op jit(solution)/shard_map/pallas_call | solution.py:464
  121.7 1.3 %copy.11 = f32[128,4096]{1,0:T(8,128)} copy(f32[128,4096]{1,0:T(8,128)S(1)} %shard_map.55) | data formatting | bytes 4194304
  (1 shorter events, 0.0 us)
Async XLA Ops:
  2.9 1.6 %copy-start = (f32[128,4096]{1,0:T(8,128)S(1)}, f32[128,4096]{1,0:T(8,128)}, u32[]{:S(2)}) copy-start(f32[128,4096]{1,0:T(8,128)} %x_ref.1) | copy-start | bytes 6291460
  4.5 0.7 copy-start.1
